TPU v7x, 256 devices: a whole 4x4x8 slice. The times are simulated.
256 devices in a mesh: shard: 32 (over z, y), grp: 8 (over x, core).
Axes of the slice: x: 4, y: 4, z: 8, core: 2. Of those that a mesh axis runs over, the one named last changes fastest.
Arguments:
- queries: bfloat16 [8192, 32, 128], P(('shard', 'grp')), may hold values from -0.5 to 0.5
- candidates: int32 [8192, 32], P(('shard', 'grp')), may hold values from 0 to 32767, as said below
- passages: bfloat16 [32768, 128, 128], P(('shard', 'grp')), may hold values from -6 to 6
Outputs:
- scores: float32 [8192, 32], P(('shard', 'grp'))
Inputs may be any that keep to these rules, and one draw needn't show every extreme that they name: Passage p is held by the device p // 128 in shard+grp order. One device, the same for all, holds exactly 8 of the 1024 candidates of every device's queries; every other device holds at most 7 of the candidates of any one device's queries.
All inputs are finite; a program needn't handle non-finite values.
Results may differ from a plain program's by a relative error of at most 0.0003.
Values may be sent and summed in bfloat16 or wider, within the bound.
A program may use at most 192 MiB of HBM per device.

v0:
```python
import math

import jax
import jax.numpy as jnp
from jax import lax
from jax.sharding import PartitionSpec as P


def score_rows(block_rows, doc_rows, q_tokens):
    similar = jnp.einsum("bid,bjd->bij", block_rows, doc_rows, preferred_element_type=jnp.float32)
    return jnp.sum(jnp.max(similar, axis=2), axis=1) / q_tokens


def local(queries, candidates, passages):
    shards = lax.axis_size("shard")
    groups = lax.axis_size("grp")
    device_count = shards * groups
    q_local, n_cand = candidates.shape
    pair_count = q_local * n_cand
    capacity = 2 * pair_count // device_count
    per_device = passages.shape[0]
    flat_ids = candidates.reshape(pair_count)
    holder = flat_ids // per_device
    local_index = flat_ids % per_device
    hits = (holder[:, None] == jnp.arange(device_count, dtype=jnp.int32)[None, :]).astype(jnp.int32)
    ranking = jnp.sum(jnp.cumsum(hits, axis=0) * hits, axis=1) - 1
    slot = holder * capacity + ranking
    q_tokens = queries.shape[1]
    features = queries.shape[2]
    width = q_tokens * features
    pair_rows = jnp.repeat(queries.reshape(q_local, width), n_cand, axis=0)
    slot_total = device_count * capacity
    outgoing = jnp.zeros((slot_total, width), jnp.bfloat16).at[slot].set(pair_rows)
    wanted = jnp.zeros((slot_total,), jnp.int32).at[slot].set(local_index)
    outgoing = outgoing.reshape(shards, groups, capacity, width)
    wanted = wanted.reshape(shards, groups, capacity)
    arrived, targets = (
        lax.all_to_all(
            lax.all_to_all(outgoing, "shard", split_axis=0, concat_axis=0, tiled=True),
            "grp",
            split_axis=1,
            concat_axis=1,
            tiled=True,
        ),
        lax.all_to_all(
            lax.all_to_all(wanted, "shard", split_axis=0, concat_axis=0, tiled=True),
            "grp",
            split_axis=1,
            concat_axis=1,
            tiled=True,
        ),
    )
    block = math.gcd(slot_total, 128)
    query_blocks = arrived.reshape(slot_total // block, block, q_tokens, features)
    target_blocks = targets.reshape(slot_total // block, block)

    def score_block(pieces):
        block_rows, block_picks = pieces
        return score_rows(block_rows, passages[block_picks], q_tokens)

    slot_scores = lax.map(score_block, (query_blocks, target_blocks)).reshape(
        shards, groups, capacity
    )
    returned = lax.all_to_all(
        lax.all_to_all(slot_scores, "shard", split_axis=0, concat_axis=0, tiled=True),
        "grp",
        split_axis=1,
        concat_axis=1,
        tiled=True,
    )
    returned = returned.reshape(slot_total)
    return returned[slot].reshape(q_local, n_cand)


def solution(mesh):
    in_specs = (
        P(("shard", "grp"), None, None),
        P(("shard", "grp"), None),
        P(("shard", "grp"), None, None),
    )
    out_specs = P(("shard", "grp"), None)
    return jax.shard_map(local, mesh=mesh, in_specs=in_specs, out_specs=out_specs, check_vma=False)
```

profile of v0, /device:TPU:2, one launch (start us, length us, event | category | flops | bytes accessed | tf_op | source)
XLA Modules:
  0.0 880.8 jit_solution(901099633259887913)
XLA Ops:
  3.6 4.3 scatter_custom_fusion.1
  8.7 11.7 %all-to-all-start.2 = ((s32[32,8,8]{2,1,0:T(8,128)}), s32[32,8,8]{2,1,0:T(8,128)S(1)}, u32[]{:S(2)}, u32[]{:S(2)}) async-start(s32[32,8,8]{2,1,0:T(8,128)} %reshape.202), calls=%async_computation.2 | async-start | bytes 262144 | tf_op jit(solution)/shard_map/all_to_all | solution.py:46
  21.4 4.3 broadcast_in_dim.22
  25.7 22.0 %scatter_custom_fusion = bf16[2048,4096]{1,0:T(8,128)(2,1)} fusion(s32[1024]{0:T(1024)S(1)} %bitcast.56, bf16[1024,4096]{1,0:T(8,128)(2,1)} %bitcast.48, bf16[]{:T(256)} %constant.58.clone.1), kind=kCustom, calls=%fused_computation.12 | custom fusion | bytes 16777728 | tf_op jit(solution)/shard_map/scatter | solution.py:33
  47.7 9.7 %all-to-all-start = ((bf16[32,8,8,4096]{3,2,1,0:T(8,128)(2,1)}), bf16[32,8,8,4096]{3,2,1,0:T(8,128)(2,1)}, u32[]{:S(2)}, u32[]{:S(2)}) async-start(bf16[32,8,8,4096]{3,2,1,0:T(8,128)(2,1)} %bitcast.45), calls=%async_computation | async-start | bytes 33554432 | tf_op jit(solution)/shard_map/all_to_all | solution.py:39
  58.2 382.9 %all-to-all-done = bf16[32,8,8,4096]{3,2,1,0:T(8,128)(2,1)} async-done(((bf16[32,8,8,4096]{3,2,1,0:T(8,128)(2,1)}), bf16[32,8,8,4096]{3,2,1,0:T(8,128)(2,1)}, u32[]{:S(2)}, u32[]{:S(2)}) %all-to-all-start) | async-done | bytes 16777248 | tf_op jit(solution)/shard_map/all_to_all | solution.py:39
  441.1 4.8 all-to-all-start.3
  445.9 14.0 %copy.32 = bf16[32,8,8,4096]{3,2,0,1:T(8,128)(2,1)} copy(bf16[32,8,8,4096]{3,2,1,0:T(8,128)(2,1)} %all-to-all-done) | data formatting | bytes 33554432 | tf_op jit(solution)/shard_map/all_to_all | solution.py:39
  459.9 5.7 all-to-all-start.1
  467.2 181.5 %all-to-all-done.1 = bf16[32,8,8,4096]{3,2,0,1:T(8,128)(2,1)} async-done(((bf16[32,8,8,4096]{3,2,0,1:T(8,128)(2,1)}), bf16[32,8,8,4096]{3,2,0,1:T(8,128)(2,1)}, u32[]{:S(2)}, u32[]{:S(2)}) %all-to-all-start.1) | async-done | bytes 16777248 | tf_op jit(solution)/shard_map/all_to_all | solution.py:38
  648.7 8.2 copy.33
  656.9 7.9 copy.40
  664.8 164.7 %while.10 = (s32[]{:T(128)}, f32[16,128]{1,0:T(8,128)S(1)}, bf16[16,128,32,128]{3,2,1,0:T(8,128)(2,1)}, s32[16,128]{1,0:T(8,128)S(1)}, bf16[128,128,128]{2,1,0:T(8,128)(2,1)}, /*index=5*/s32[]{:T(128)}, f32[]{:T(128)}, s32[]{:T(128)}) while((s32[]{:T(128)}, f32[16,128]{1,0:T(8,128)S(1)}, bf16[16,128,32,128]{3,2,1,0:T(8,128)(2,1)}, ...), condition=%wide.region_8.9_spmd, body=%wide.region_5.8_spmd.sunk | while | flops 134743424 | bytes 13673569 | solution.py:61
  664.8 5.2 gather_fusion
  670.0 4.9 convolution_reduce_fusion.2
  675.1 5.2 gather_fusion
  680.3 4.9 convolution_reduce_fusion.2
  685.4 5.2 gather_fusion
  690.6 4.9 convolution_reduce_fusion.2
  695.7 5.2 gather_fusion
  700.9 4.9 convolution_reduce_fusion.2
  706.0 5.2 gather_fusion
  711.2 4.9 convolution_reduce_fusion.2
  716.3 5.2 gather_fusion
  721.5 4.9 convolution_reduce_fusion.2
  726.6 5.2 gather_fusion
  731.8 4.9 convolution_reduce_fusion.2
  736.9 5.2 gather_fusion
  742.1 4.9 convolution_reduce_fusion.2
  747.2 5.2 gather_fusion
  752.4 4.9 convolution_reduce_fusion.2
  757.5 5.2 gather_fusion
  762.7 4.9 convolution_reduce_fusion.2
  767.8 5.2 gather_fusion
  773.0 4.9 convolution_reduce_fusion.2
  778.1 5.2 gather_fusion
  783.3 4.9 convolution_reduce_fusion.2
  788.4 5.2 gather_fusion
  793.6 4.9 convolution_reduce_fusion.2
  798.7 5.2 gather_fusion
  803.8 4.9 convolution_reduce_fusion.2
  808.9 5.2 gather_fusion
  814.1 4.9 convolution_reduce_fusion.2
  819.2 5.2 gather_fusion
  824.4 4.9 convolution_reduce_fusion.2
  829.6 33.5 %all_to_all.30 = f32[32,8,8]{2,1,0:T(8,128)S(1)} all-to-all(f32[32,8,8]{2,1,0:T(8,128)S(1)} %reshape.204), channel_id=1, replica_groups=mesh['shard'=32,'grp'=8] {'shard'}, dimensions={0} | all-to-all | bytes 16384 | tf_op jit(solution)/shard_map/all_to_all | solution.py:65
  863.9 4.7 all-to-all-start.5
  874.0 6.2 gather_fusion.1
  (118 shorter events, 17.3 us)
Async XLA Ops:
  8.7 39.0 %all-to-all-start.2 = ((s32[32,8,8]{2,1,0:T(8,128)}), s32[32,8,8]{2,1,0:T(8,128)S(1)}, u32[]{:S(2)}, u32[]{:S(2)}) async-start(s32[32,8,8]{2,1,0:T(8,128)} %reshape.202), calls=%async_computation.2 | async-start | bytes 262144 | tf_op jit(solution)/shard_map/all_to_all | solution.py:46
  47.7 393.4 %all-to-all-start = ((bf16[32,8,8,4096]{3,2,1,0:T(8,128)(2,1)}), bf16[32,8,8,4096]{3,2,1,0:T(8,128)(2,1)}, u32[]{:S(2)}, u32[]{:S(2)}) async-start(bf16[32,8,8,4096]{3,2,1,0:T(8,128)(2,1)} %bitcast.45), calls=%async_computation | async-start | bytes 33554432 | tf_op jit(solution)/shard_map/all_to_all | solution.py:39
  441.1 18.8 %all-to-all-start.3 = ((s32[8,1,256]{2,1,0:T(1,128)}), s32[8,1,256]{2,1,0:T(1,128)S(1)}, u32[]{:S(2)}, u32[]{:S(2)}) async-start(s32[8,1,256]{2,1,0:T(1,128)} %reshape.243), calls=%async_computation.3 | async-start | bytes 16384 | tf_op jit(solution)/shard_map/all_to_all | solution.py:45
  459.9 188.8 %all-to-all-start.1 = ((bf16[32,8,8,4096]{3,2,0,1:T(8,128)(2,1)}), bf16[32,8,8,4096]{3,2,0,1:T(8,128)(2,1)}, u32[]{:S(2)}, u32[]{:S(2)}) async-start(bf16[32,8,8,4096]{3,2,0,1:T(8,128)(2,1)} %copy.32), calls=%async_computation.1 | async-start | bytes 33554432 | tf_op jit(solution)/shard_map/all_to_all | solution.py:38
  863.9 8.6 all-to-all-start.5
where the time goes:
time: 884 us; the launch traced here: 881 us
  waiting for transfers between devices  568 us (64%)
  local copies, waits for them, and re-layouts  159 us (18%)
  matrix products  78 us (9%)
  starting transfers between devices  36.6 us (4%)
  blocking collectives  33.5 us (4%)
    all_to_all x1, waiting for transfers between devices, local(): lax.all_to_all(outgoing, 'shard', split_axis=0, concat_axis=0, tiled=True)  383 us
    all_to_all x1, waiting for transfers between devices, local(): lax.all_to_all(lax.all_to_all(outgoing, 'shard', split_axis=0, concat_axi...  182 us
    gather x16, local copies, waits for them, and re-layouts, score_block(): return score_rows(block_rows, passages[block_picks], q_tokens)  83.2 us
    dot_general x16, matrix products, score_rows(): jnp.einsum('bid,bjd->bij', block_rows, doc_rows, preferred_element_type=j...  78 us
    all_to_all x1, blocking collectives, local(): lax.all_to_all(slot_scores, 'shard', split_axis=0, concat_axis=0, tiled=T...  33.5 us
    scatter x1, local copies, waits for them, and re-layouts, local(): jnp.zeros((slot_total, width), jnp.bfloat16).at[slot].set(pair_rows)  22 us
  transfers between devices with their start and end apart: 5, of which 3 were waited for; matrix products, arithmetic and copies ran while one was open for 5% of the time, Pallas kernels for 0%

commit v1 on v0

v1 whole, which is shorter than its diff:
```python
import functools

import jax
import jax.numpy as jnp
from jax import lax
from jax.experimental import pallas as pl
from jax.experimental.pallas import tpu as pltpu
from jax.sharding import PartitionSpec as P

MESH = pl.DeviceIdType.MESH
NZ, NY, NX = 8, 4, 4
PLANE = NY * NX
CHIPS = NZ * PLANE
QN, QTOK, DIM, DTOK = 32, 32, 128, 128
HALF = QTOK // 2
PAIRS = 1024
P_DEV = 128
SLOTS = 15
LINE = 16


def coords():
    shard, grp = lax.axis_index("shard"), lax.axis_index("grp")
    return shard // NY, shard % NY, grp // 2, grp % 2


def place(z, y, x, c):
    return (z * NY + y, x * 2 + c)


def table_kernel(cand_ref, table_ref, rank_ref):
    cand = cand_ref[...]
    chip = cand // (2 * P_DEV)
    within = cand % (2 * P_DEV)
    onehot = (lax.broadcasted_iota(jnp.int32, (CHIPS, PAIRS), 0) == chip).astype(jnp.bfloat16)
    before = (
        lax.broadcasted_iota(jnp.int32, (128, 128), 0)
        < lax.broadcasted_iota(jnp.int32, (128, 128), 1)
    ).astype(jnp.bfloat16)
    carry = jnp.zeros((CHIPS, 1), jnp.float32)
    ranks = []
    for b in range(PAIRS // 128):
        block = onehot[:, b * 128 : (b + 1) * 128]
        count = jnp.dot(block, before, preferred_element_type=jnp.float32) + carry
        wide = block.astype(jnp.float32)
        ranks.append(jnp.sum(wide * count, axis=0, keepdims=True))
        carry = carry + jnp.sum(wide, axis=1, keepdims=True)
    rank = jnp.concatenate(ranks, axis=1).astype(jnp.int32)
    rank_ref[...] = rank
    lane = (chip % PLANE) * LINE + rank
    spread = (lax.broadcasted_iota(jnp.int32, (PLANE * LINE, PAIRS), 0) == lane).astype(jnp.bfloat16)
    at_z = lax.broadcasted_iota(jnp.int32, (NZ, PAIRS), 0) == chip // PLANE
    query = lax.broadcasted_iota(jnp.int32, (NZ, PAIRS), 1) // QN
    dims = (((1,), (1,)), ((), ()))
    picked = [
        lax.dot_general(
            jnp.where(at_z, value, 0).astype(jnp.float32).astype(jnp.bfloat16),
            spread,
            dims,
            preferred_element_type=jnp.float32,
        ).astype(jnp.int32)
        for value in (query, jnp.broadcast_to(within, (NZ, PAIRS)))
    ]
    table = picked[0] * 256 + picked[1]
    table_ref[:, 0, :] = table[:, :128]
    table_ref[:, 1, :] = table[:, 128:]


def offset_z(t):
    return jnp.where(t % 2 == 0, t // 2, NZ - (t + 1) // 2)


def offset_j(j):
    return jnp.where(j >= 2, 5 - j, j)


def main_kernel(
    q_ref, table_ref, pas_hbm, out_ref,
    ga, gb, sa, sb, ra, rb, pas, stage_a, stage_b, t_line, t_plane, tbl, s_own, s_line,
    ax_send, ax_recv, z_send, z_recv, p_send, p_recv,
    tl_send, tl_recv, tp_send, tp_recv, sl_send, sl_recv, sp_send, sp_recv, pas_sem, loc_sem,
):
    z, y, x, c = coords()
    chip = y * NX + x
    plane = [(dy, dx) for dy in range(NY) for dx in range(NX) if (dy, dx) != (0, 0)]

    def to_z(dz):
        return place((z + dz) % NZ, y, x, c)

    def to_plane(dy, dx):
        return place(z, (y + dy) % NY, (x + dx) % NX, c)

    def copy(src, dst, send, recv, device):
        return pltpu.make_async_remote_copy(
            src_ref=src, dst_ref=dst, send_sem=send, recv_sem=recv, device_id=device, device_id_type=MESH
        )

    sibling = place(z, y, x, 1 - c)
    barrier = pltpu.get_barrier_semaphore()
    everyone = [to_z(dz) for dz in range(1, NZ)] + [to_plane(dy, dx) for dy, dx in plane] + [sibling]
    for device in everyone:
        pl.semaphore_signal(barrier, inc=1, device_id=device, device_id_type=MESH)
    pl.semaphore_wait(barrier, len(everyone))

    def table_line(dz):
        return copy(table_ref.at[(z + dz) % NZ], t_line.at[z], tl_send.at[dz - 1], tl_recv.at[dz - 1], to_z(dz))

    for dz in range(1, NZ):
        table_line(dz).start()
    t_line[z] = table_ref[z]

    def axis_a(o):
        return copy(q_ref.at[:, :HALF], ga.at[z, y], ax_send.at[0, o - 1], ax_recv.at[0, o - 1], to_plane(o, 0))

    def axis_b(o):
        return copy(q_ref.at[:, HALF:], gb.at[z, x], ax_send.at[1, o - 1], ax_recv.at[1, o - 1], to_plane(0, o))

    for o in (1, 3, 2):
        axis_a(o).start()
        axis_b(o).start()
    ga[z, y] = q_ref[:, :HALF]
    gb[z, x] = q_ref[:, HALF:]

    own_pas = pltpu.make_async_copy(pas_hbm, pas.at[pl.ds(c * P_DEV, P_DEV)], loc_sem.at[0])
    own_pas.start()
    their_pas = copy(pas_hbm, pas.at[pl.ds(c * P_DEV, P_DEV)], pas_sem.at[0], pas_sem.at[1], sibling)
    their_pas.start()

    s_own[...] = jnp.zeros_like(s_own)

    def ring(part, t, j, up, late):
        zs = (z + offset_z(t)) % NZ
        buf, sub = (ga, (y + offset_j(j)) % NY) if part == 0 else (gb, (x + offset_j(j)) % NX)
        return copy(
            buf.at[zs, sub], buf.at[zs, sub],
            z_send.at[up, part, t, j], z_recv.at[part, late, j],
            to_z(1 if up else NZ - 1),
        )

    def ring_start(t, j):
        @pl.when(t == 0)
        def _():
            for part in range(2):
                ring(part, t, j, 1, 1).start()
                ring(part, t, j, 0, 2).start()

        for up in range(2):
            @pl.when((t >= 1) & (t <= 4) & (t % 2 == up))
            def _(up=up):
                for part in range(2):
                    ring(part, t, j, up, t + 2).start()

        @pl.when(t == 5)
        def _():
            ring(0, t, j, 1, 7).start()

        @pl.when(t == 6)
        def _():
            ring(1, t, j, 0, 7).start()

    def packed(part, t, j, o):
        zs = (z + offset_z(t)) % NZ
        if part == 0:
            ys = (y + offset_j(j)) % NY
            return copy(
                sa.at[o - 1, t, j], ra.at[zs, ys, x],
                p_send.at[part, t, j, o - 1], p_recv.at[part, t, j, o - 1], to_plane(0, o),
            )
        xs = (x + offset_j(j)) % NX
        return copy(
            sb.at[o - 1, t, j], rb.at[zs, y, xs],
            p_send.at[part, t, j, o - 1], p_recv.at[part, t, j, o - 1], to_plane(o, 0),
        )

    def arrive(t, j):
        @pl.when((t == 0) & (j > 0))
        def _():
            o = offset_j(j)
            for part, buf, sub in ((0, ga, (y + o) % NY), (1, gb, (x + o) % NX)):
                here = buf.at[z, sub]
                copy(here, here, ax_send.at[part, 3 - o], ax_recv.at[part, 3 - o], sibling).wait_recv()

        @pl.when(t > 0)
        def _():
            zs = (z + offset_z(t)) % NZ
            for part, buf, sub in ((0, ga, (y + offset_j(j)) % NY), (1, gb, (x + offset_j(j)) % NX)):
                here = buf.at[zs, sub]
                copy(here, here, z_send.at[0, part, t, j], z_recv.at[part, t, j], sibling).wait_recv()

    def process(t, j):
        zs = (z + offset_z(t)) % NZ
        ys = (y + offset_j(j)) % NY
        xs = (x + offset_j(j)) % NX
        arrive(t, j)
        ring_start(t, j)
        stage_a[...] = ga[zs, ys]
        stage_b[...] = gb[zs, xs]
        for o in (2, 1, 3, 0):
            for part in range(2):
                if part == 0:
                    src, dst, stage = ys * NX + x, y * NX + (x + o) % NX, stage_a
                else:
                    src, dst, stage = y * NX + xs, ((y + o) % NY) * NX + x, stage_b
                for k in range(SLOTS):
                    row = tbl[src, zs, dst // 8, (dst % 8) * LINE + k] // 256
                    value = stage[row]
                    if o > 0:
                        (sa if part == 0 else sb)[o - 1, t, j, k] = value
                    elif part == 0:
                        ra[zs, ys, x, k] = value
                    else:
                        rb[zs, y, xs, k] = value
                if o > 0:
                    packed(part, t, j, o).start()

    lanes = lax.broadcasted_iota(jnp.int32, (8, 128), 1)

    def wait_packed(t):
        @pl.loop(0, 4)
        def _(j):
            for o in range(1, 4):
                for part in range(2):
                    packed_here(part, t, j, o).wait_recv()

    def packed_here(part, t, j, o):
        zs = (z + offset_z(t)) % NZ
        if part == 0:
            here = ra.at[zs, (y + offset_j(j)) % NY, (x + 4 - o) % NX]
        else:
            here = rb.at[zs, (y + 4 - o) % NY, (x + offset_j(j)) % NX]
        return copy(here, here, p_send.at[part, t, j, o - 1], p_recv.at[part, t, j, o - 1], sibling)

    def compute(m):
        t, ys = m // 4, m % 4
        zs = (z + offset_z(t)) % NZ

        @pl.when(ys == 0)
        def _():
            wait_packed(t)

        def source(xs, acc):
            for k in range(SLOTS):
                query = jnp.concatenate([ra[zs, ys, xs, k], rb[zs, ys, xs, k]], axis=0)
                passage = pas[tbl[ys * NX + xs, zs, chip // 8, (chip % 8) * LINE + k] % 256]
                similar = lax.dot_general(
                    query, passage, (((1,), (1,)), ((), ())), preferred_element_type=jnp.float32
                )
                best = jnp.max(similar, axis=1, keepdims=True)
                part = best[0:8] + best[8:16] + best[16:24] + best[24:32]
                acc = jnp.where(lanes == (ys % 2) * 64 + xs * LINE + k, part, acc)
            return acc

        acc = lax.fori_loop(0, NX, source, jnp.zeros((8, 128), jnp.float32))
        row = pl.ds(ys // 2, 1)
        s_own[zs, row] = s_own[zs, row] + jnp.sum(acc, axis=0, keepdims=True) * (1.0 / QTOK)

    for dz in range(1, NZ):
        here = t_line.at[(z + NZ - dz) % NZ]
        copy(here, here, tl_send.at[dz - 1], tl_recv.at[dz - 1], sibling).wait_recv()
    for i, (dy, dx) in enumerate(plane):
        copy(t_line, t_plane.at[chip], tp_send.at[i], tp_recv.at[i], to_plane(dy, dx)).start()
    t_plane[chip] = t_line[...]
    for i, (dy, dx) in enumerate(plane):
        here = t_plane.at[((y + NY - dy) % NY) * NX + (x + NX - dx) % NX]
        copy(here, here, tp_send.at[i], tp_recv.at[i], sibling).wait_recv()
    to_scalar = pltpu.make_async_copy(t_plane, tbl, loc_sem.at[1])
    to_scalar.start()
    to_scalar.wait()

    def unit(u):
        v = jnp.clip(u - 4, 0, 23)
        middle = (u >= 4) & (u < 28)
        t = jnp.where(middle, 2 * (v // 8) + 1 + v % 2, jnp.where(u < 4, 0, 7))
        j = jnp.where(middle, (v % 8) // 2, u % 4)
        process(t, j)

    @pl.loop(0, 8)
    def _(u):
        unit(u)

    own_pas.wait()
    their_pas.wait()

    @pl.loop(8, 28)
    def _(u):
        unit(u)
        compute(u - 8)

    @pl.loop(28, 32)
    def _(u):
        unit(u)

        @pl.loop(0, 2)
        def _(i):
            compute(20 + 2 * (u - 28) + i)

    @pl.loop(28, 32)
    def _(m):
        compute(m)

    for dz in range(1, NZ):
        copy(s_own.at[(z + dz) % NZ], s_line.at[z], sl_send.at[dz - 1], sl_recv.at[dz - 1], to_z(dz)).start()
    s_line[z] = s_own[z]
    for dz in range(1, NZ):
        here = s_line.at[(z + NZ - dz) % NZ]
        copy(here, here, sl_send.at[dz - 1], sl_recv.at[dz - 1], sibling).wait_recv()
    for i, (dy, dx) in enumerate(plane):
        copy(s_line, out_ref.at[chip], sp_send.at[i], sp_recv.at[i], to_plane(dy, dx)).start()
    out_ref[chip] = s_line[...]
    for i, (dy, dx) in enumerate(plane):
        here = out_ref.at[((y + NY - dy) % NY) * NX + (x + NX - dx) % NX]
        copy(here, here, sp_send.at[i], sp_recv.at[i], sibling).wait_recv()

    for dz in range(1, NZ):
        table_line(dz).wait_send()
        copy(s_own.at[(z + dz) % NZ], s_line.at[z], sl_send.at[dz - 1], sl_recv.at[dz - 1], to_z(dz)).wait_send()
    for o in (1, 2, 3):
        axis_a(o).wait_send()
        axis_b(o).wait_send()
    for i, (dy, dx) in enumerate(plane):
        copy(t_line, t_plane.at[chip], tp_send.at[i], tp_recv.at[i], to_plane(dy, dx)).wait_send()
        copy(s_line, out_ref.at[chip], sp_send.at[i], sp_recv.at[i], to_plane(dy, dx)).wait_send()

    @pl.loop(0, 4)
    def _(j):
        for part in range(2):
            ring(part, 0, j, 1, 1).wait_send()
            ring(part, 0, j, 0, 2).wait_send()
            for t in range(1, 5):
                ring(part, t, j, t % 2, t + 2).wait_send()
        ring(0, 5, j, 1, 7).wait_send()
        ring(1, 6, j, 0, 7).wait_send()

    @pl.loop(0, 32)
    def _(n):
        for o in range(1, 4):
            for part in range(2):
                packed(part, n // 4, n % 4, o).wait_send()


def scatter_kernel(d_ref, cand_ref, rank_ref, out_ref):
    _, y, x, _ = coords()
    mine = y * NX + x
    chip = cand_ref[...] // (2 * P_DEV)
    low = d_ref[:, :, 0, :].reshape(CHIPS, 128)
    high = d_ref[:, :, 1, :].reshape(CHIPS, 128)
    rows = jnp.where(mine // 8 == 0, low, high)
    rows = pltpu.roll(rows, (128 - (mine % 8) * LINE) % 128, 1)
    by_slot = rows.T[:LINE]
    holder = (chip % PLANE) * NZ + chip // PLANE
    onehot = (lax.broadcasted_iota(jnp.int32, (CHIPS, PAIRS), 0) == holder).astype(jnp.bfloat16)
    total = jnp.zeros((LINE, PAIRS), jnp.float32)
    left = by_slot
    for _ in range(3):
        piece = left.astype(jnp.bfloat16)
        left = left - piece.astype(jnp.float32)
        total = total + jnp.dot(piece, onehot, preferred_element_type=jnp.float32)
    pick = lax.broadcasted_iota(jnp.int32, (LINE, PAIRS), 0) == rank_ref[...]
    out_ref[...] = jnp.sum(jnp.where(pick, total, 0.0), axis=0, keepdims=True)


def local(queries, candidates, passages):
    vmem = pl.BlockSpec(memory_space=pltpu.VMEM)
    cand = candidates.reshape(1, PAIRS)
    table, rank = pl.pallas_call(
        table_kernel,
        out_shape=(
            jax.ShapeDtypeStruct((NZ, 2, 128), jnp.int32),
            jax.ShapeDtypeStruct((1, PAIRS), jnp.int32),
        ),
        in_specs=[vmem],
        out_specs=(vmem, vmem),
    )(cand)
    bf16, f32, i32 = jnp.bfloat16, jnp.float32, jnp.int32
    dma = pltpu.SemaphoreType.DMA
    returned = pl.pallas_call(
        main_kernel,
        out_shape=jax.ShapeDtypeStruct((PLANE, NZ, 2, 128), f32),
        in_specs=[vmem, vmem, pl.BlockSpec(memory_space=pl.ANY)],
        out_specs=vmem,
        scratch_shapes=[
            pltpu.VMEM((NZ, NY, QN, HALF, DIM), bf16),
            pltpu.VMEM((NZ, NX, QN, HALF, DIM), bf16),
            pltpu.VMEM((3, NZ, 4, SLOTS, HALF, DIM), bf16),
            pltpu.VMEM((3, NZ, 4, SLOTS, HALF, DIM), bf16),
            pltpu.VMEM((NZ, NY, NX, SLOTS, HALF, DIM), bf16),
            pltpu.VMEM((NZ, NY, NX, SLOTS, HALF, DIM), bf16),
            pltpu.VMEM((2 * P_DEV, DTOK, DIM), bf16),
            pltpu.VMEM((QN, HALF, DIM), bf16),
            pltpu.VMEM((QN, HALF, DIM), bf16),
            pltpu.VMEM((NZ, 2, 128), i32),
            pltpu.VMEM((PLANE, NZ, 2, 128), i32),
            pltpu.SMEM((PLANE, NZ, 2, 128), i32),
            pltpu.VMEM((NZ, 2, 128), f32),
            pltpu.VMEM((NZ, 2, 128), f32),
            dma((2, 3)), dma((2, 3)),
            dma((2, 2, 8, 4)), dma((2, 8, 4)),
            dma((2, 8, 4, 3)), dma((2, 8, 4, 3)),
            dma((NZ - 1,)), dma((NZ - 1,)),
            dma((PLANE - 1,)), dma((PLANE - 1,)),
            dma((NZ - 1,)), dma((NZ - 1,)),
            dma((PLANE - 1,)), dma((PLANE - 1,)),
            dma((2,)), dma((2,)),
        ],
        compiler_params=pltpu.CompilerParams(
            collective_id=0, has_side_effects=True, vmem_limit_bytes=60 * 2**20
        ),
    )(queries, table, passages)
    scores = pl.pallas_call(
        scatter_kernel,
        out_shape=jax.ShapeDtypeStruct((1, PAIRS), f32),
        in_specs=[vmem, vmem, vmem],
        out_specs=vmem,
    )(returned, cand, rank)
    return scores.reshape(QN, PAIRS // QN)


def solution(mesh):
    in_specs = (
        P(("shard", "grp"), None, None),
        P(("shard", "grp"), None),
        P(("shard", "grp"), None, None),
    )
    out_specs = P(("shard", "grp"), None)
    return jax.shard_map(local, mesh=mesh, in_specs=in_specs, out_specs=out_specs, check_vma=False)
```

time: 884 us -> 152 us (0.17)
  waiting for transfers between devices: 568 us -> 0 us
  local copies, waits for them, and re-layouts: 159 us -> 2.65 us
  Pallas kernels: 0 us -> 147 us
  matrix products: 78 us -> 0 us
  starting transfers between devices: 36.6 us -> 0 us
  blocking collectives: 33.5 us -> 0 us
    all_to_all x5 -> x0, waiting for transfers between devices: 568 us -> none  [the longest x1 383 us: local(): lax.all_to_all(outgoing, 'shard', split_axis=0, concat_axis=0, tiled=True)]
    pallas_call x0 -> x3, Pallas kernels: none -> 147 us  [the longest x1 143 us: local(): pl.pallas_call(main_kernel, out_shape=jax.ShapeDtypeStruct((PLANE, NZ, 2,...]
    gather x17 -> x0, local copies, waits for them, and re-layouts: 89.3 us -> none  [the longest x16 83.2 us: score_block(): return score_rows(block_rows, passages[block_picks], q_tokens)]
    dot_general x16 -> x0, matrix products: 78 us -> none  [score_rows(): jnp.einsum('bid,bjd->bij', block_rows, doc_rows, preferred_element_type=j...]
    all_to_all x5 -> x0, starting transfers between devices: 36.6 us -> none  [the longest x1 11.7 us: local(): lax.all_to_all(wanted, 'shard', split_axis=0, concat_axis=0, tiled=True)]
    all_to_all x1 -> x0, blocking collectives: 33.5 us -> none  [local(): lax.all_to_all(slot_scores, 'shard', split_axis=0, concat_axis=0, tiled=T...]
    scatter x2 -> x0, local copies, waits for them, and re-layouts: 26.3 us -> none  [the longest x1 22 us: local(): jnp.zeros((slot_total, width), jnp.bfloat16).at[slot].set(pair_rows)]
    all_to_all x8 -> x0, local copies, waits for them, and re-layouts: 23.7 us -> none  [the longest x1 14 us: local(): lax.all_to_all(outgoing, 'shard', split_axis=0, concat_axis=0, tiled=True)]
  transfers between devices with their start and end apart: 5 -> 0, of which waited for: 3 -> 0; matrix products, arithmetic and copies ran while one was open for 5% -> 0% of each run, Pallas kernels for 0% -> 0%
where the time goes in v1:
time: 152 us; the launch traced here: 151 us
  Pallas kernels  147 us (97%)
  local copies, waits for them, and re-layouts  2.65 us (2%)
    pallas_call x1, Pallas kernels, local(): pl.pallas_call(main_kernel, out_shape=jax.ShapeDtypeStruct((PLANE, NZ, 2,...  143 us

profile of v1, /device:TPU:2, one launch (start us, length us, event | category | flops | bytes accessed | tf_op | source)
XLA Modules:
  0.0 151.3 jit_solution(1692311086830567079)
XLA Ops:
  0.0 1.4 reshape.6.cand_ref
  1.4 1.9 %shard_map.37 = (s32[8,2,128]{2,1,0:T(2,128)}, s32[1,1024]{1,0:T(1,128)}) custom-call(s32[1,1024]{1,0:T(1,128)} %reshape.6.cand_ref), custom_call_target="tpu_custom_call" | custom-call | tf_op jit(solution)/shard_map/pallas_call | solution.py:365
  3.3 143.4 %shard_map.38.d_ref = f32[16,8,2,128]{3,2,1,0:T(2,128)} custom-call(bf16[32,32,128]{2,1,0:T(8,128)(2,1)} %q_ref.1, s32[8,2,128]{2,1,0:T(2,128)} %get-tuple-element.7.table_ref, bf16[128,128,128]{2,1,0:T(8,128)(2,1)} %pas_hbm.1), custom_call_target="tpu_custom_call" | custom-call | tf_op jit(solution)/shard_map/pallas_call | solution.py:376
  146.7 1.9 %shard_map.39 = f32[1,1024]{1,0:T(1,128)} custom-call(f32[16,8,2,128]{3,2,1,0:T(2,128)} %shard_map.38.d_ref, s32[1,1024]{1,0:T(1,128)} %reshape.6.cand_ref, s32[1,1024]{1,0:T(1,128)} %get-tuple-element.8.rank_ref), custom_call_target="tpu_custom_call" | custom-call | tf_op jit(solution)/shard_map/pallas_call | solution.py:409
  148.6 0.6 broadcast.3
  149.2 1.4 reduce.3
  150.6 0.7 reshape.7

commit v2 on v1

v2 whole, which is shorter than its diff:
```python
import jax
import jax.numpy as jnp
from jax import lax
from jax.experimental import pallas as pl
from jax.experimental.pallas import tpu as pltpu
from jax.sharding import PartitionSpec as P

MESH = pl.DeviceIdType.MESH
NZ, NY, NX = 8, 4, 4
PLANE = NY * NX
CHIPS = NZ * PLANE
QN, QTOK, DIM, DTOK = 32, 32, 128, 128
HALF = QTOK // 2
PAIRS = 1024
P_DEV = 128
SLOTS = 15
LINE = 16


def coords():
    shard, grp = lax.axis_index("shard"), lax.axis_index("grp")
    return shard // NY, shard % NY, grp // 2, grp % 2


def place(z, y, x, c):
    return (z * NY + y, x * 2 + c)


def pair_rows(cand_ref):
    wide = jnp.concatenate([cand_ref[pl.ds(r, 8, stride=4), :] for r in range(4)], axis=1)
    return [wide[b : b + 1] for b in range(PAIRS // 128)]


def holders(rows):
    chips = lax.broadcasted_iota(jnp.int32, (CHIPS, 128), 0)
    return [(chips == row // (2 * P_DEV)).astype(jnp.float32) for row in rows]


def slot_tables(cand_ref, table_ref, rank_ref):
    rows = pair_rows(cand_ref)
    before = (
        lax.broadcasted_iota(jnp.int32, (128, 128), 0)
        < lax.broadcasted_iota(jnp.int32, (128, 128), 1)
    ).astype(jnp.bfloat16)
    carry = jnp.zeros((CHIPS, 1), jnp.float32)
    totals = [jnp.zeros((NZ, PLANE * LINE), jnp.float32) for _ in range(2)]
    for b, (row, onehot) in enumerate(zip(rows, holders(rows))):
        count = jnp.dot(onehot.astype(jnp.bfloat16), before, preferred_element_type=jnp.float32) + carry
        rank = jnp.sum(onehot * count, axis=0, keepdims=True).astype(jnp.int32)
        carry = carry + jnp.sum(onehot, axis=1, keepdims=True)
        rank_ref[b : b + 1] = rank
        chip, within = row // (2 * P_DEV), row % (2 * P_DEV)
        lane = (chip % PLANE) * LINE + rank
        spread = (lax.broadcasted_iota(jnp.int32, (PLANE * LINE, 128), 0) == lane).astype(jnp.float32)
        at_z = lax.broadcasted_iota(jnp.int32, (NZ, 128), 0) == chip // PLANE
        query = (lax.broadcasted_iota(jnp.int32, (NZ, 128), 1) + b * 128) // QN
        for n, value in enumerate((query, jnp.broadcast_to(within, (NZ, 128)))):
            totals[n] = totals[n] + lax.dot_general(
                jnp.where(at_z, value, 0).astype(jnp.float32).astype(jnp.bfloat16),
                spread.astype(jnp.bfloat16),
                (((1,), (1,)), ((), ())),
                preferred_element_type=jnp.float32,
            )
    table = totals[0].astype(jnp.int32) * 256 + totals[1].astype(jnp.int32)
    table_ref[:, 0, :] = table[:, :128]
    table_ref[:, 1, :] = table[:, 128:]


def scores_to_pairs(cand_ref, rank_ref, landed_ref, out_ref):
    by_slot = landed_ref[...].reshape(CHIPS, 128).T[:LINE]
    pieces = []
    for _ in range(3):
        pieces.append(by_slot.astype(jnp.bfloat16))
        by_slot = by_slot - pieces[-1].astype(jnp.float32)
    rows = pair_rows(cand_ref)
    done = []
    for b, onehot in enumerate(holders(rows)):
        onehot = onehot.astype(jnp.bfloat16)
        total = sum(jnp.dot(p, onehot, preferred_element_type=jnp.float32) for p in pieces)
        pick = lax.broadcasted_iota(jnp.int32, (LINE, 128), 0) == rank_ref[b : b + 1]
        done.append(jnp.sum(jnp.where(pick, total, 0.0), axis=0, keepdims=True))
    wide = jnp.concatenate(done, axis=0)
    for r in range(4):
        out_ref[pl.ds(r, 8, stride=4), :] = wide[:, r * QN : (r + 1) * QN]


def offset_z(t):
    return jnp.where(t % 2 == 0, t // 2, NZ - (t + 1) // 2)


def offset_j(j):
    return jnp.where(j >= 2, 5 - j, j)


def main_kernel(
    q_ref, cand_ref, pas_hbm, out_ref,
    ga, gb, sa, sb, ra, rb, pas, stage_a, stage_b,
    t_own, t_near, t_line, t_plane, tbl_near, tbl, rank_ref, scored, landed,
    ax_send, ax_recv, z_send, z_recv, p_send, p_recv,
    tn_send, tn_recv, tl_send, tl_recv, tp_send, tp_recv, home_sem, pas_sem, loc_sem,
):
    z, y, x, c = coords()
    chip = y * NX + x
    plane = [(dy, dx) for dy in range(NY) for dx in range(NX) if (dy, dx) != (0, 0)]

    def to_z(dz):
        return place((z + dz) % NZ, y, x, c)

    def to_plane(dy, dx):
        return place(z, (y + dy) % NY, (x + dx) % NX, c)

    def copy(src, dst, send, recv, device):
        return pltpu.make_async_remote_copy(
            src_ref=src, dst_ref=dst, send_sem=send, recv_sem=recv, device_id=device, device_id_type=MESH
        )

    sibling = place(z, y, x, 1 - c)
    barrier = pltpu.get_barrier_semaphore()
    everyone = [to_z(dz) for dz in range(1, NZ)] + [to_plane(dy, dx) for dy, dx in plane] + [sibling]
    for device in everyone:
        pl.semaphore_signal(barrier, inc=1, device_id=device, device_id_type=MESH)
    own_pas = pltpu.make_async_copy(pas_hbm, pas.at[pl.ds(c * P_DEV, P_DEV)], loc_sem.at[0])
    own_pas.start()
    ga[z, y] = q_ref[:, :HALF]
    gb[z, x] = q_ref[:, HALF:]
    slot_tables(cand_ref, t_own, rank_ref)
    t_near[chip] = t_own[z]
    t_line[z] = t_own[z]
    pl.semaphore_wait(barrier, len(everyone))

    def table_near(i):
        return copy(t_own.at[z], t_near.at[chip], tn_send.at[i], tn_recv.at[i], to_plane(*plane[i]))

    def table_line(dz):
        return copy(t_own.at[(z + dz) % NZ], t_line.at[z], tl_send.at[dz - 1], tl_recv.at[dz - 1], to_z(dz))

    def table_plane(i):
        return copy(t_line, t_plane.at[chip], tp_send.at[i], tp_recv.at[i], to_plane(*plane[i]))

    for i in range(PLANE - 1):
        table_near(i).start()
    for dz in range(1, NZ):
        table_line(dz).start()

    def axis_a(o):
        return copy(q_ref.at[:, :HALF], ga.at[z, y], ax_send.at[0, o - 1], ax_recv.at[0, o - 1], to_plane(o, 0))

    def axis_b(o):
        return copy(q_ref.at[:, HALF:], gb.at[z, x], ax_send.at[1, o - 1], ax_recv.at[1, o - 1], to_plane(0, o))

    for o in (1, 3, 2):
        axis_a(o).start()
        axis_b(o).start()

    their_pas = copy(pas_hbm, pas.at[pl.ds(c * P_DEV, P_DEV)], pas_sem.at[0], pas_sem.at[1], sibling)
    their_pas.start()

    def ring(part, t, j, up, late):
        zs = (z + offset_z(t)) % NZ
        buf, sub = (ga, (y + offset_j(j)) % NY) if part == 0 else (gb, (x + offset_j(j)) % NX)
        return copy(
            buf.at[zs, sub], buf.at[zs, sub],
            z_send.at[up, part, t, j], z_recv.at[part, late, j],
            to_z(1 if up else NZ - 1),
        )

    def ring_start(t, j):
        @pl.when(t == 0)
        def _():
            for part in range(2):
                ring(part, t, j, 1, 1).start()
                ring(part, t, j, 0, 2).start()

        for up in range(2):
            @pl.when((t >= 1) & (t <= 4) & (t % 2 == up))
            def _(up=up):
                for part in range(2):
                    ring(part, t, j, up, t + 2).start()

        @pl.when(t == 5)
        def _():
            ring(0, t, j, 1, 7).start()

        @pl.when(t == 6)
        def _():
            ring(1, t, j, 0, 7).start()

    def packed(part, t, j, o):
        zs = (z + offset_z(t)) % NZ
        if part == 0:
            ys = (y + offset_j(j)) % NY
            return copy(
                sa.at[o - 1, t, j], ra.at[zs, ys, x],
                p_send.at[part, t, j, o - 1], p_recv.at[part, t, j, o - 1], to_plane(0, o),
            )
        xs = (x + offset_j(j)) % NX
        return copy(
            sb.at[o - 1, t, j], rb.at[zs, y, xs],
            p_send.at[part, t, j, o - 1], p_recv.at[part, t, j, o - 1], to_plane(o, 0),
        )

    def arrive(t, j):
        @pl.when((t == 0) & (j > 0))
        def _():
            o = offset_j(j)
            for part, buf, sub in ((0, ga, (y + o) % NY), (1, gb, (x + o) % NX)):
                here = buf.at[z, sub]
                copy(here, here, ax_send.at[part, 3 - o], ax_recv.at[part, 3 - o], sibling).wait_recv()

        @pl.when(t > 0)
        def _():
            zs = (z + offset_z(t)) % NZ
            for part, buf, sub in ((0, ga, (y + offset_j(j)) % NY), (1, gb, (x + offset_j(j)) % NX)):
                here = buf.at[zs, sub]
                copy(here, here, z_send.at[0, part, t, j], z_recv.at[part, t, j], sibling).wait_recv()

    def process(t, j, near):
        zs = (z + offset_z(t)) % NZ
        ys = (y + offset_j(j)) % NY
        xs = (x + offset_j(j)) % NX
        arrive(t, j)
        ring_start(t, j)
        stage_a[...] = ga[zs, ys]
        stage_b[...] = gb[zs, xs]
        for o in (2, 1, 3, 0):
            for part in range(2):
                if part == 0:
                    src, dst, stage = ys * NX + x, y * NX + (x + o) % NX, stage_a
                else:
                    src, dst, stage = y * NX + xs, ((y + o) % NY) * NX + x, stage_b
                for k in range(SLOTS):
                    lane = (dst % 8) * LINE + k
                    word = tbl_near[src, dst // 8, lane] if near else tbl[src, zs, dst // 8, lane]
                    value = stage[(word >> 8) & (QN - 1)]
                    if o > 0:
                        (sa if part == 0 else sb)[o - 1, t, j, k] = value
                    elif part == 0:
                        ra[zs, ys, x, k] = value
                    else:
                        rb[zs, y, xs, k] = value
                if o > 0:
                    packed(part, t, j, o).start()

    lanes = lax.broadcasted_iota(jnp.int32, (1, 128), 1)

    def home(zs, ys, xs):
        to = (zs * NY + ys) * NX + xs
        return copy(scored.at[to], landed.at[z * PLANE + chip], home_sem.at[0], home_sem.at[1], place(zs, ys, xs, c))

    def compute(m):
        t = m // 4
        zs = (z + offset_z(t)) % NZ
        where = []
        for i in range(4):
            n = 4 * (m % 4) + i
            shell = jnp.where(n >= 9, 3, jnp.where(n >= 4, 2, jnp.where(n >= 1, 1, 0)))
            step = n - shell * shell
            a, b = jnp.minimum(step, shell), jnp.minimum(2 * shell - step, shell)
            ys, xs = (y + offset_j(a)) % NY, (x + offset_j(b)) % NX
            where.append((ys, xs))

            @pl.when(b != 0)
            def _(t=t, a=a, b=b, ys=ys, xs=xs):
                here, o = ra.at[zs, ys, xs], 3 - offset_j(b)
                copy(here, here, p_send.at[0, t, a, o], p_recv.at[0, t, a, o], sibling).wait_recv()

            @pl.when(a != 0)
            def _(t=t, a=a, b=b, ys=ys, xs=xs):
                here, o = rb.at[zs, ys, xs], 3 - offset_j(a)
                copy(here, here, p_send.at[1, t, b, o], p_recv.at[1, t, b, o], sibling).wait_recv()

        for i, (ys, xs) in enumerate(where):
            acc = jnp.zeros((1, 128), jnp.float32)
            for k in range(SLOTS):
                query = jnp.concatenate([ra[zs, ys, xs, k], rb[zs, ys, xs, k]], axis=0)
                passage = pas[tbl[ys * NX + xs, zs, chip // 8, (chip % 8) * LINE + k] & (2 * P_DEV - 1)]
                similar = lax.dot_general(
                    passage, query, (((1,), (1,)), ((), ())), preferred_element_type=jnp.float32
                )
                best = jnp.max(similar, axis=0, keepdims=True)
                acc = jnp.where(lanes == k, jnp.sum(best, axis=1, keepdims=True) * (1.0 / QTOK), acc)
            scored[(zs * NY + ys) * NX + xs] = acc

        for i, (ys, xs) in enumerate(where):
            @pl.when((m > 0) | (i > 0))
            def _(ys=ys, xs=xs):
                home(zs, ys, xs).start()

    for dz in range(1, NZ):
        here = t_line.at[(z + NZ - dz) % NZ]
        copy(here, here, tl_send.at[dz - 1], tl_recv.at[dz - 1], sibling).wait_recv()
    for i in range(PLANE - 1):
        table_plane(i).start()
    t_plane[chip] = t_line[...]

    def from_plane(i):
        dy, dx = plane[i]
        return ((y + NY - dy) % NY) * NX + (x + NX - dx) % NX

    for i in range(PLANE - 1):
        here = t_near.at[from_plane(i)]
        copy(here, here, tn_send.at[i], tn_recv.at[i], sibling).wait_recv()
    to_scalar = pltpu.make_async_copy(t_near, tbl_near, loc_sem.at[1])
    to_scalar.start()
    to_scalar.wait()

    @pl.loop(0, 4)
    def _(j):
        process(0, j, True)

    for i in range(PLANE - 1):
        here = t_plane.at[from_plane(i)]
        copy(here, here, tp_send.at[i], tp_recv.at[i], sibling).wait_recv()
    to_scalar = pltpu.make_async_copy(t_plane, tbl, loc_sem.at[1])
    to_scalar.start()
    to_scalar.wait()

    def unit(u):
        v = jnp.minimum(u - 4, 23)
        middle = u < 28
        t = jnp.where(middle, 2 * (v // 8) + 1 + v % 2, 7)
        j = jnp.where(middle, (v % 8) // 2, u % 4)
        process(t, j, False)

    @pl.loop(4, 8)
    def _(u):
        unit(u)

    own_pas.wait()
    their_pas.wait()

    @pl.loop(8, 28)
    def _(u):
        unit(u)
        compute(u - 8)

    @pl.loop(28, 32)
    def _(u):
        unit(u)

        @pl.loop(0, 2)
        def _(i):
            compute(20 + 2 * (u - 28) + i)

    @pl.loop(28, 32)
    def _(m):
        compute(m)

    own = z * PLANE + chip
    landed[own] = scored[own]
    others = pl.ds(0, CHIPS - 1)
    copy(scored.at[others], landed.at[others], home_sem.at[0], home_sem.at[1], sibling).wait()
    scores_to_pairs(cand_ref, rank_ref, landed, out_ref)

    for dz in range(1, NZ):
        table_line(dz).wait_send()
    for o in (1, 2, 3):
        axis_a(o).wait_send()
        axis_b(o).wait_send()
    for i in range(PLANE - 1):
        table_near(i).wait_send()
        table_plane(i).wait_send()

    @pl.loop(0, 4)
    def _(j):
        for part in range(2):
            ring(part, 0, j, 1, 1).wait_send()
            ring(part, 0, j, 0, 2).wait_send()
            for t in range(1, 5):
                ring(part, t, j, t % 2, t + 2).wait_send()
        ring(0, 5, j, 1, 7).wait_send()
        ring(1, 6, j, 0, 7).wait_send()

    @pl.loop(0, 32)
    def _(n):
        for o in range(1, 4):
            for part in range(2):
                packed(part, n // 4, n % 4, o).wait_send()


def local(queries, candidates, passages):
    vmem = pl.BlockSpec(memory_space=pltpu.VMEM)
    bf16, f32, i32 = jnp.bfloat16, jnp.float32, jnp.int32
    dma = pltpu.SemaphoreType.DMA
    return pl.pallas_call(
        main_kernel,
        out_shape=jax.ShapeDtypeStruct(candidates.shape, f32),
        in_specs=[vmem, vmem, pl.BlockSpec(memory_space=pl.ANY)],
        out_specs=vmem,
        scratch_shapes=[
            pltpu.VMEM((NZ, NY, QN, HALF, DIM), bf16),
            pltpu.VMEM((NZ, NX, QN, HALF, DIM), bf16),
            pltpu.VMEM((3, NZ, 4, SLOTS, HALF, DIM), bf16),
            pltpu.VMEM((3, NZ, 4, SLOTS, HALF, DIM), bf16),
            pltpu.VMEM((NZ, NY, NX, SLOTS, HALF, DIM), bf16),
            pltpu.VMEM((NZ, NY, NX, SLOTS, HALF, DIM), bf16),
            pltpu.VMEM((2 * P_DEV, DTOK, DIM), bf16),
            pltpu.VMEM((QN, HALF, DIM), bf16),
            pltpu.VMEM((QN, HALF, DIM), bf16),
            pltpu.VMEM((NZ, 2, 128), i32),
            pltpu.VMEM((PLANE, 2, 128), i32),
            pltpu.VMEM((NZ, 2, 128), i32),
            pltpu.VMEM((PLANE, NZ, 2, 128), i32),
            pltpu.SMEM((PLANE, 2, 128), i32),
            pltpu.SMEM((PLANE, NZ, 2, 128), i32),
            pltpu.VMEM((PAIRS // 128, 128), i32),
            pltpu.VMEM((CHIPS, 1, 128), f32),
            pltpu.VMEM((CHIPS, 1, 128), f32),
            dma((2, 3)), dma((2, 3)),
            dma((2, 2, 8, 4)), dma((2, 8, 4)),
            dma((2, 8, 4, 3)), dma((2, 8, 4, 3)),
            dma((PLANE - 1,)), dma((PLANE - 1,)),
            dma((NZ - 1,)), dma((NZ - 1,)),
            dma((PLANE - 1,)), dma((PLANE - 1,)),
            dma((2,)), dma((2,)), dma((2,)),
        ],
        compiler_params=pltpu.CompilerParams(
            collective_id=0, has_side_effects=True, vmem_limit_bytes=60 * 2**20
        ),
    )(queries, candidates, passages)


def solution(mesh):
    in_specs = (
        P(("shard", "grp"), None, None),
        P(("shard", "grp"), None),
        P(("shard", "grp"), None, None),
    )
    out_specs = P(("shard", "grp"), None)
    return jax.shard_map(local, mesh=mesh, in_specs=in_specs, out_specs=out_specs, check_vma=False)
```

time: 152 us -> 122 us (0.80)
  Pallas kernels: 147 us -> 120 us
    pallas_call x3 -> x1, Pallas kernels: 147 us -> 120 us  [local(): pl.pallas_call(main_kernel, out_shape=jax.ShapeDtypeStruct(candidates.sha...]
    reshape x2 -> x0, local copies, waits for them, and re-layouts: 2.06 us -> none  [the longest x1 1.38 us: local(): cand = candidates.reshape(1, PAIRS)]
where the time goes in v2:
time: 122 us; the launch traced here: 121 us
  Pallas kernels  120 us (98%)
  local copies, waits for them, and re-layouts  1.32 us (1%)
    pallas_call x1, Pallas kernels, local(): pl.pallas_call(main_kernel, out_shape=jax.ShapeDtypeStruct(candidates.sha...  120 us

profile of v2, /device:TPU:2, one launch (start us, length us, event | category | flops | bytes accessed | tf_op | source)
XLA Modules:
  0.0 121.3 jit_solution(5582309432904655309)
XLA Ops:
  0.0 120.0 %shard_map.37 = f32[32,32]{1,0:T(8,128)} custom-call(bf16[32,32,128]{2,1,0:T(8,128)(2,1)} %q_ref.1, s32[32,32]{1,0:T(8,128)} %cand_ref.1, bf16[128,128,128]{2,1,0:T(8,128)(2,1)} %pas_hbm.1), custom_call_target="tpu_custom_call" | custom-call | tf_op jit(solution)/shard_map/pallas_call | solution.py:385
  120.0 1.3 %copy.5 = f32[32,32]{1,0:T(8,128)} copy(f32[32,32]{1,0:T(8,128)} %shard_map.37) | data formatting | bytes 8192

commit v3 on v2

v3 whole, which is shorter than its diff:
```python
import jax
import jax.numpy as jnp
from jax import lax
from jax.experimental import pallas as pl
from jax.experimental.pallas import tpu as pltpu
from jax.sharding import PartitionSpec as P

MESH = pl.DeviceIdType.MESH
NZ, NY, NX = 8, 4, 4
PLANE = NY * NX
CHIPS = NZ * PLANE
QN, QTOK, DIM, DTOK = 32, 32, 128, 128
HALF = QTOK // 2
PAIRS = 1024
P_DEV = 128
SLOTS = 15
LINE = 16

HUBS = ((0, 0), (0, 2), (2, 1), (2, 3))
STEPS = (
    ((0, 1), (1, 0), (3, 0)),
    ((0, 1), (1, 0), (3, 0)),
    ((3, 0), (0, 3), (1, 0)),
    ((3, 0), (0, 3), (1, 0)),
)


def swapped(offset, part):
    return offset if part == 0 else offset[::-1]


def code(offset):
    return offset[0] * NX + offset[1]


HUB = [[code(swapped(h, p)) for h in HUBS] for p in range(2)]
STEP = [[[code(swapped(STEPS[j][n], p)) for j in range(4)] for n in range(3)] for p in range(2)]
REACH = [
    [
        [
            code(swapped(((HUBS[j][0] + STEPS[j][n][0]) % NY, (HUBS[j][1] + STEPS[j][n][1]) % NX), p))
            for j in range(4)
        ]
        for n in range(3)
    ]
    for p in range(2)
]
SERVER = [[0] * 16 for _ in range(2)]
for _p in range(2):
    for _j in range(4):
        SERVER[_p][HUB[_p][_j]] = _j
        for _n in range(3):
            SERVER[_p][REACH[_p][_n][_j]] = _j
LAST = [max(SERVER[0][d], SERVER[1][d]) for d in range(16)]
ORDER = sorted(range(16), key=lambda d: (LAST[d], d))
NEEDS = [min(i for i in range(4) if max(LAST[d] for d in ORDER[4 * i : 4 * i + 4]) >= j) for j in range(4)]


def look(values, n):
    words = []
    for start in (0, 8):
        word = sum(v << (4 * i) for i, v in enumerate(values[start : start + 8]))
        words.append(word - 2**32 if word >= 2**31 else word)
    if len(values) <= 8:
        return (jnp.int32(words[0]) >> (4 * n)) & 15
    return (jnp.where(n < 8, jnp.int32(words[0]), jnp.int32(words[1])) >> (4 * (n % 8))) & 15


def coords():
    shard, grp = lax.axis_index("shard"), lax.axis_index("grp")
    return shard // NY, shard % NY, grp // 2, grp % 2


def place(z, y, x, c):
    return (z * NY + y, x * 2 + c)


def pair_rows(cand_ref):
    wide = jnp.concatenate([cand_ref[pl.ds(r, 8, stride=4), :] for r in range(4)], axis=1)
    return [wide[b : b + 1] for b in range(PAIRS // 128)]


def holders(rows):
    chips = lax.broadcasted_iota(jnp.int32, (CHIPS, 128), 0)
    return [(chips == row // (2 * P_DEV)).astype(jnp.float32) for row in rows]


def slot_tables(cand_ref, table_ref, rank_ref):
    rows = pair_rows(cand_ref)
    before = (
        lax.broadcasted_iota(jnp.int32, (128, 128), 0)
        < lax.broadcasted_iota(jnp.int32, (128, 128), 1)
    ).astype(jnp.bfloat16)
    carry = jnp.zeros((CHIPS, 1), jnp.float32)
    totals = [jnp.zeros((NZ, PLANE * LINE), jnp.float32) for _ in range(2)]
    for b, (row, onehot) in enumerate(zip(rows, holders(rows))):
        count = jnp.dot(onehot.astype(jnp.bfloat16), before, preferred_element_type=jnp.float32) + carry
        rank = jnp.sum(onehot * count, axis=0, keepdims=True).astype(jnp.int32)
        carry = carry + jnp.sum(onehot, axis=1, keepdims=True)
        rank_ref[b : b + 1] = rank
        chip, within = row // (2 * P_DEV), row % (2 * P_DEV)
        lane = (chip % PLANE) * LINE + rank
        spread = (lax.broadcasted_iota(jnp.int32, (PLANE * LINE, 128), 0) == lane).astype(jnp.float32)
        at_z = lax.broadcasted_iota(jnp.int32, (NZ, 128), 0) == chip // PLANE
        query = (lax.broadcasted_iota(jnp.int32, (NZ, 128), 1) + b * 128) // QN
        for n, value in enumerate((query, jnp.broadcast_to(within, (NZ, 128)))):
            totals[n] = totals[n] + lax.dot_general(
                jnp.where(at_z, value, 0).astype(jnp.float32).astype(jnp.bfloat16),
                spread.astype(jnp.bfloat16),
                (((1,), (1,)), ((), ())),
                preferred_element_type=jnp.float32,
            )
    table = totals[0].astype(jnp.int32) * 256 + totals[1].astype(jnp.int32)
    table_ref[:, 0, :] = table[:, :128]
    table_ref[:, 1, :] = table[:, 128:]


def scores_to_pairs(cand_ref, rank_ref, landed_ref, out_ref):
    by_slot = landed_ref[...].reshape(CHIPS, 128).T[:LINE]
    pieces = []
    for _ in range(3):
        pieces.append(by_slot.astype(jnp.bfloat16))
        by_slot = by_slot - pieces[-1].astype(jnp.float32)
    rows = pair_rows(cand_ref)
    done = []
    for b, onehot in enumerate(holders(rows)):
        onehot = onehot.astype(jnp.bfloat16)
        total = sum(jnp.dot(p, onehot, preferred_element_type=jnp.float32) for p in pieces)
        pick = lax.broadcasted_iota(jnp.int32, (LINE, 128), 0) == rank_ref[b : b + 1]
        done.append(jnp.sum(jnp.where(pick, total, 0.0), axis=0, keepdims=True))
    wide = jnp.concatenate(done, axis=0)
    for r in range(4):
        out_ref[pl.ds(r, 8, stride=4), :] = wide[:, r * QN : (r + 1) * QN]


def offset_z(t):
    return jnp.where(t % 2 == 0, t // 2, NZ - (t + 1) // 2)


def main_kernel(
    q_ref, cand_ref, pas_hbm, out_ref,
    ga, gb, sa, sb, ra, rb, pas, stage_a, stage_b,
    t_own, t_near, t_line, t_plane, tbl_near, tbl, rank_ref, scored, landed,
    ax_send, ax_recv, z_send, z_recv, p_send, p_recv,
    tn_send, tn_recv, tl_send, tl_recv, tp_send, tp_recv, home_sem, pas_sem, loc_sem,
):
    z, y, x, c = coords()
    chip = y * NX + x
    plane = [(dy, dx) for dy in range(NY) for dx in range(NX) if (dy, dx) != (0, 0)]

    def to_z(dz):
        return place((z + dz) % NZ, y, x, c)

    def to_plane(dy, dx):
        return place(z, (y + dy) % NY, (x + dx) % NX, c)

    def copy(src, dst, send, recv, device):
        return pltpu.make_async_remote_copy(
            src_ref=src, dst_ref=dst, send_sem=send, recv_sem=recv, device_id=device, device_id_type=MESH
        )

    sibling = place(z, y, x, 1 - c)

    def drain(like, sem):
        pltpu.make_async_copy(like, like, sem).wait()

    barrier = pltpu.get_barrier_semaphore()
    everyone = [to_z(dz) for dz in range(1, NZ)] + [to_plane(dy, dx) for dy, dx in plane] + [sibling]
    for device in everyone:
        pl.semaphore_signal(barrier, inc=1, device_id=device, device_id_type=MESH)
    own_pas = pltpu.make_async_copy(pas_hbm, pas.at[pl.ds(c * P_DEV, P_DEV)], loc_sem.at[0])
    own_pas.start()
    ga[0, 0] = q_ref[:, :HALF]
    gb[0, 0] = q_ref[:, HALF:]
    slot_tables(cand_ref, t_own, rank_ref)
    t_near[chip] = t_own[z]
    t_line[z] = t_own[z]
    pl.semaphore_wait(barrier, len(everyone))

    def table_near(i):
        return copy(t_own.at[z], t_near.at[chip], tn_send.at[0], tn_recv.at[0], to_plane(*plane[i]))

    def table_line(dz):
        return copy(t_own.at[(z + dz) % NZ], t_line.at[z], tl_send.at[0], tl_recv.at[0], to_z(dz))

    def table_plane(i):
        return copy(t_line, t_plane.at[chip], tp_send.at[0], tp_recv.at[0], to_plane(*plane[i]))

    for i in range(PLANE - 1):
        table_near(i).start()
    for dz in range(1, NZ):
        table_line(dz).start()

    def shifted(offset, sign=1):
        return (y + sign * (offset // NX) + NY) % NY, (x + sign * (offset % NX) + NX) % NX

    def at(offset):
        ys, xs = shifted(offset)
        return place(z, ys, xs, c)

    def spread(part, j):
        return copy(
            q_ref.at[:, part * HALF : (part + 1) * HALF], (ga, gb)[part].at[0, j],
            ax_send.at[0], ax_recv.at[j], at(HUB[part][j]),
        )

    def spread_start(j):
        spread(0, j).start()
        spread(1, j).start()

    spread_start(1)

    their_pas = copy(pas_hbm, pas.at[pl.ds(c * P_DEV, P_DEV)], pas_sem.at[0], pas_sem.at[1], sibling)
    their_pas.start()

    def ring(part, t, j, up, late):
        buf = (ga, gb)[part]
        return copy(
            buf.at[t, j], buf.at[late, j],
            z_send.at[part], z_recv.at[late, j],
            to_z(1 if up else NZ - 1),
        )

    def ring_start(t, j):
        @pl.when(t == 0)
        def _():
            for part in range(2):
                ring(part, t, j, 1, 1).start()
                ring(part, t, j, 0, 2).start()

        for up in range(2):
            @pl.when((t >= 1) & (t <= 4) & (t % 2 == up))
            def _(up=up):
                for part in range(2):
                    ring(part, t, j, up, t + 2).start()

        @pl.when(t == 5)
        def _():
            ring(0, t, j, 1, 7).start()

        @pl.when(t == 6)
        def _():
            ring(1, t, j, 0, 7).start()

    def packed(part, t, j, n):
        return copy(
            (sa, sb)[part].at[n, t, j], (ra, rb)[part].at[t, look(REACH[part][n], j)],
            p_send.at[part], p_recv.at[t, j], at(look(STEP[part][n], j)),
        )

    def arrive(t, j):
        @pl.when((t == 0) & (j > 0))
        def _():
            drain(ga.at[0, pl.ds(0, 2)], ax_recv.at[j])

        @pl.when(t > 0)
        def _():
            drain(ga.at[t, pl.ds(0, 2)], z_recv.at[t, j])

    def process(t, j, near):
        zs = (z + offset_z(t)) % NZ
        stage_a[...] = ga[t, j]
        stage_b[...] = gb[t, j]
        for n in range(4):
            for part in range(2):
                hub = look(HUB[part], j)
                ys, xs = shifted(hub, -1)
                src = ys * NX + xs
                if n < 3:
                    ys, xs = shifted(look(STEP[part][n], j))
                    dst, put, where = ys * NX + xs, (sa, sb)[part], (n, t, j)
                else:
                    dst, put, where = chip, (ra, rb)[part], (t, hub)
                stage = (stage_a, stage_b)[part]
                row, lane = dst // 8, (dst % 8) * LINE
                for k in range(SLOTS):
                    word = tbl_near[src, row, lane + k] if near else tbl[src, zs, row, lane + k]
                    put[(*where, k)] = stage[(word >> 8) & (QN - 1)]
                if n < 3:
                    packed(part, t, j, n).start()

    lanes = lax.broadcasted_iota(jnp.int32, (1, 128), 1)

    def home(zs, ys, xs):
        to = (zs * NY + ys) * NX + xs
        return copy(scored.at[to], landed.at[z * PLANE + chip], home_sem.at[0], home_sem.at[1], place(zs, ys, xs, c))

    def compute(m):
        t = m // 4
        zs = (z + offset_z(t)) % NZ
        where = []
        for i in range(4):
            offset = look(ORDER, 4 * (m % 4) + i)
            where.append((offset, *shifted(offset, -1)))

        for j in range(4):
            @pl.when(look(NEEDS, j) == m % 4)
            def _(j=j):
                drain(ra.at[t, pl.ds(0, 6)], p_recv.at[t, j])

        for offset, ys, xs in where:
            acc = jnp.zeros((1, 128), jnp.float32)
            for k in range(SLOTS):
                query = jnp.concatenate([ra[t, offset, k], rb[t, offset, k]], axis=0)
                word = tbl[ys * NX + xs, zs, chip // 8, (chip % 8) * LINE + k]
                passage = pas[word & (2 * P_DEV - 1)]
                similar = lax.dot_general(
                    passage, query, (((1,), (1,)), ((), ())), preferred_element_type=jnp.float32
                )
                best = jnp.max(similar, axis=0, keepdims=True)
                acc = jnp.where(lanes == k, jnp.sum(best, axis=1, keepdims=True) * (1.0 / QTOK), acc)
            scored[(zs * NY + ys) * NX + xs] = acc

        for i, (_, ys, xs) in enumerate(where):
            @pl.when((m > 0) | (i > 0))
            def _(ys=ys, xs=xs):
                home(zs, ys, xs).start()

    ring_start(0, 0)

    drain(t_line.at[pl.ds(0, NZ - 1)], tl_recv.at[0])
    spread_start(2)
    for i in range(PLANE - 1):
        table_plane(i).start()
    t_plane[chip] = t_line[...]

    arrive(0, 1)
    spread_start(3)
    ring_start(0, 1)

    drain(t_near.at[pl.ds(0, PLANE - 1)], tn_recv.at[0])
    to_scalar = pltpu.make_async_copy(t_near, tbl_near, loc_sem.at[1])
    to_scalar.start()
    to_scalar.wait()

    @pl.loop(0, 4)
    def _(j):
        @pl.when(j >= 2)
        def _():
            arrive(0, j)
            ring_start(0, j)

        process(0, j, True)

    drain(t_plane.at[pl.ds(0, PLANE - 1)], tp_recv.at[0])
    to_scalar = pltpu.make_async_copy(t_plane, tbl, loc_sem.at[1])
    to_scalar.start()
    to_scalar.wait()

    def unit(u):
        v = jnp.minimum(u - 4, 23)
        middle = u < 28
        t = jnp.where(middle, 2 * (v // 8) + 1 + v % 2, 7)
        j = jnp.where(middle, (v % 8) // 2, u % 4)
        arrive(t, j)
        ring_start(t, j)
        process(t, j, False)

    @pl.loop(4, 8)
    def _(u):
        unit(u)

    own_pas.wait()
    their_pas.wait()

    @pl.loop(8, 28)
    def _(u):
        unit(u)
        compute(u - 8)

    @pl.loop(28, 32)
    def _(u):
        unit(u)

        @pl.loop(0, 2)
        def _(i):
            compute(20 + 2 * (u - 28) + i)

    @pl.loop(28, 32)
    def _(m):
        compute(m)

    own = z * PLANE + chip
    landed[own] = scored[own]
    others = pl.ds(0, CHIPS - 1)
    copy(scored.at[others], landed.at[others], home_sem.at[0], home_sem.at[1], sibling).wait()
    scores_to_pairs(cand_ref, rank_ref, landed, out_ref)

    drain(t_near.at[pl.ds(0, PLANE - 1)], tn_send.at[0])
    drain(t_line.at[pl.ds(0, NZ - 1)], tl_send.at[0])
    drain(t_plane.at[pl.ds(0, PLANE - 1)], tp_send.at[0])
    drain(ga.at[0, pl.ds(0, 3)], ax_send.at[0])
    drain(gb.at[0, pl.ds(0, 3)], ax_send.at[0])
    drain(ga.at[pl.ds(0, NZ - 1)], z_send.at[0])
    drain(gb.at[pl.ds(0, NZ - 1)], z_send.at[1])
    drain(sa, p_send.at[0])
    drain(sb, p_send.at[1])


def local(queries, candidates, passages):
    vmem = pl.BlockSpec(memory_space=pltpu.VMEM)
    bf16, f32, i32 = jnp.bfloat16, jnp.float32, jnp.int32
    dma = pltpu.SemaphoreType.DMA
    return pl.pallas_call(
        main_kernel,
        out_shape=jax.ShapeDtypeStruct(candidates.shape, f32),
        in_specs=[vmem, vmem, pl.BlockSpec(memory_space=pl.ANY)],
        out_specs=vmem,
        scratch_shapes=[
            pltpu.VMEM((NZ, 4, QN, HALF, DIM), bf16),
            pltpu.VMEM((NZ, 4, QN, HALF, DIM), bf16),
            pltpu.VMEM((3, NZ, 4, SLOTS, HALF, DIM), bf16),
            pltpu.VMEM((3, NZ, 4, SLOTS, HALF, DIM), bf16),
            pltpu.VMEM((NZ, PLANE, SLOTS, HALF, DIM), bf16),
            pltpu.VMEM((NZ, PLANE, SLOTS, HALF, DIM), bf16),
            pltpu.VMEM((2 * P_DEV, DTOK, DIM), bf16),
            pltpu.VMEM((QN, HALF, DIM), bf16),
            pltpu.VMEM((QN, HALF, DIM), bf16),
            pltpu.VMEM((NZ, 2, 128), i32),
            pltpu.VMEM((PLANE, 2, 128), i32),
            pltpu.VMEM((NZ, 2, 128), i32),
            pltpu.VMEM((PLANE, NZ, 2, 128), i32),
            pltpu.SMEM((PLANE, 2, 128), i32),
            pltpu.SMEM((PLANE, NZ, 2, 128), i32),
            pltpu.VMEM((PAIRS // 128, 128), i32),
            pltpu.VMEM((CHIPS, 1, 128), f32),
            pltpu.VMEM((CHIPS, 1, 128), f32),
            dma((1,)), dma((4,)),
            dma((2,)), dma((8, 4)),
            dma((2,)), dma((8, 4)),
            dma((1,)), dma((1,)), dma((1,)), dma((1,)), dma((1,)), dma((1,)),
            dma((2,)), dma((2,)), dma((2,)),
        ],
        compiler_params=pltpu.CompilerParams(
            collective_id=0, has_side_effects=True, vmem_limit_bytes=60 * 2**20
        ),
    )(queries, candidates, passages)


def solution(mesh):
    in_specs = (
        P(("shard", "grp"), None, None),
        P(("shard", "grp"), None),
        P(("shard", "grp"), None, None),
    )
    out_specs = P(("shard", "grp"), None)
    return jax.shard_map(local, mesh=mesh, in_specs=in_specs, out_specs=out_specs, check_vma=False)
```

time: 122 us -> 112 us (0.918)
  Pallas kernels: 120 us -> 110 us
    pallas_call x1, Pallas kernels: 120 us -> 110 us  [local(): pl.pallas_call(main_kernel, out_shape=jax.ShapeDtypeStruct(candidates.sha...]
where the time goes in v3:
time: 112 us; the launch traced here: 111 us
  Pallas kernels  110 us (98%)
  local copies, waits for them, and re-layouts  1.32 us (1%)
    pallas_call x1, Pallas kernels, local(): pl.pallas_call(main_kernel, out_shape=jax.ShapeDtypeStruct(candidates.sha...  110 us

profile of v3, /device:TPU:2, one launch (start us, length us, event | category | flops | bytes accessed | tf_op | source)
XLA Modules:
  0.0 111.3 jit_solution(5820124871352397475)
XLA Ops:
  0.0 110.0 %shard_map.37 = f32[32,32]{1,0:T(8,128)} custom-call(bf16[32,32,128]{2,1,0:T(8,128)(2,1)} %q_ref.1, s32[32,32]{1,0:T(8,128)} %cand_ref.1, bf16[128,128,128]{2,1,0:T(8,128)(2,1)} %pas_hbm.1), custom_call_target="tpu_custom_call" | custom-call | tf_op jit(solution)/shard_map/pallas_call | solution.py:404
  110.0 1.3 %copy.5 = f32[32,32]{1,0:T(8,128)} copy(f32[32,32]{1,0:T(8,128)} %shard_map.37) | data formatting | bytes 8192

commit v4 on v3

--- a/solution.py
+++ b/solution.py
@@ -211,7 +211,6 @@
     spread_start(1)
 
     their_pas = copy(pas_hbm, pas.at[pl.ds(c * P_DEV, P_DEV)], pas_sem.at[0], pas_sem.at[1], sibling)
-    their_pas.start()
 
     def ring(part, t, j, up, late):
         buf = (ga, gb)[part]
@@ -328,6 +327,7 @@
     spread_start(3)
     ring_start(0, 1)
 
+    their_pas.start()
     drain(t_near.at[pl.ds(0, PLANE - 1)], tn_recv.at[0])
     to_scalar = pltpu.make_async_copy(t_near, tbl_near, loc_sem.at[1])
     to_scalar.start()

time: 112 us -> 111 us (level)
  no operation moved by 1% of the time
where the time goes in v4:
time: 111 us
  Pallas kernels  110 us (99%)
  local copies, waits for them, and re-layouts  1.32 us (1%)
    pallas_call x1, Pallas kernels, local(): pl.pallas_call(main_kernel, out_shape=jax.ShapeDtypeStruct(candidates.sha...  110 us

profile of v4, /device:TPU:2, one launch (start us, length us, event | category | flops | bytes accessed | tf_op | source)
XLA Modules:
  0.0 111.3 jit_solution(2795247420009127555)
XLA Ops:
  0.0 110.0 %shard_map.37 = f32[32,32]{1,0:T(8,128)} custom-call(bf16[32,32,128]{2,1,0:T(8,128)(2,1)} %q_ref.1, s32[32,32]{1,0:T(8,128)} %cand_ref.1, bf16[128,128,128]{2,1,0:T(8,128)(2,1)} %pas_hbm.1), custom_call_target="tpu_custom_call" | custom-call | tf_op jit(solution)/shard_map/pallas_call | solution.py:404
  110.0 1.3 %copy.5 = f32[32,32]{1,0:T(8,128)} copy(f32[32,32]{1,0:T(8,128)} %shard_map.37) | data formatting | bytes 8192
